TPU v7x, 32 devices: a whole 2x2x4 slice. The times are simulated.
32 devices in a mesh: grp: 2 (over x), row: 8 (over z, y), col: 2 (over core).
Axes of the slice: x: 2, y: 2, z: 4, core: 2. Of those that a mesh axis runs over, the one named last changes fastest.
Arguments:
- tiles: float32 [3072, 128, 128], P(('grp', 'row', 'col')), parts along dimension 0, as said below
- tile_rows: int32 [3072], P(('grp', 'row', 'col')), parts along dimension 0, may hold values from 0 to 15, as said below
- tile_cols: int32 [3072], P(('grp', 'row', 'col')), parts along dimension 0, may hold values from 0 to 127, as said below
- counts: int32 [32], P(('grp', 'row', 'col')), parts along dimension 0, may hold values from 32 to 96, as said below
- cost: float32 [65536], P(('grp', 'col')), parts along dimension 0, may hold values from -6 to 6
- lower: float32 [65536], P(('grp', 'col')), parts along dimension 0, may hold values from -1.5 to -0.1
- upper: float32 [65536], P(('grp', 'col')), parts along dimension 0, may hold values from 0.1 to 1.5
- rhs: float32 [32768], P(('grp', 'row')), parts along dimension 0, may hold values from -6 to 6
- primal_start: float32 [65536], P(('grp', 'col')), parts along dimension 0, may hold values from -3 to 3
- dual_start: float32 [32768], P(('grp', 'row')), parts along dimension 0, may hold values from 0 to 1
- step_start: float32 [2], P('grp'), parts along dimension 0, may hold values from 0.3 to 0.6
Outputs:
- primal_solution: float32 [65536], P(('grp', 'col')), parts along dimension 0
- dual_solution: float32 [32768], P(('grp', 'row')), parts along dimension 0
- row_scaling: float32 [32768], P(('grp', 'row')), parts along dimension 0
- column_scaling: float32 [65536], P(('grp', 'col')), parts along dimension 0
- step_taken: float32 [2], P('grp'), parts along dimension 0
There are 2 independent parts, one for each index of `grp`. A program takes and returns all parts, laid end to end along the dimension named above; each array names one. Nothing has to cross between parts.
Inputs may be any that keep to these rules, and one draw needn't show every extreme that they name: `tile_rows`: every tile row of the program holds at least one live tile. `tile_cols`: every tile column of the program holds at least one live tile. A device's live tiles are its first counts slots; some device has all 96 slots live in every draw. `tiles`: entries of the slots; those past a device's count are not part of the matrix.
All inputs are finite; a program needn't handle non-finite values.
Results may differ from a plain program's by a relative error of at most 0.00022.
Values sent between devices are 32-bit elements; how exact they have to be, the bound alone decides.
A program may use at most 64 MiB of HBM per device.

v0:
```python
import jax
import jax.numpy as jnp
from jax import lax
from jax.sharding import PartitionSpec as P

RUIZ = 4
ITERS = 2


EPS = 1e-06


def forward_local(tiles, tile_rows, tile_cols, live_slots, vector, row_blocks):
    tile_size = tiles.shape[1]
    pieces = vector.reshape(-1, tile_size)[tile_cols]
    product = jnp.einsum("sij,sj->si", tiles, pieces, precision=lax.Precision.HIGHEST)
    product = jnp.where(live_slots[:, None], product, 0.0)
    return jnp.zeros((row_blocks, tile_size), jnp.float32).at[tile_rows].add(product).reshape(-1)


def body(
    tiles,
    tile_rows,
    tile_cols,
    counts,
    cost,
    lower,
    upper,
    rhs,
    primal_start,
    dual_start,
    step_start,
):
    tile_size = tiles.shape[1]
    row_blocks = rhs.shape[0] // tile_size
    col_blocks = cost.shape[0] // tile_size
    live_slots = jnp.arange(tiles.shape[0], dtype=jnp.int32) < counts[0]
    magnitude = jnp.abs(tiles)
    row_scale = jnp.ones_like(rhs)
    col_scale = jnp.ones_like(cost)
    for sweep in range(RUIZ):
        col_pieces = col_scale.reshape(col_blocks, tile_size)[tile_cols]
        row_pieces = row_scale.reshape(row_blocks, tile_size)[tile_rows]
        row_part = jnp.where(
            live_slots[:, None], jnp.max(magnitude * col_pieces[:, None, :], axis=2), 0.0
        )
        col_part = jnp.where(
            live_slots[:, None], jnp.max(magnitude * row_pieces[:, :, None], axis=1), 0.0
        )
        row_local = (
            jnp.zeros((row_blocks, tile_size), jnp.float32).at[tile_rows].max(row_part).reshape(-1)
        )
        col_local = (
            jnp.zeros((col_blocks, tile_size), jnp.float32).at[tile_cols].max(col_part).reshape(-1)
        )
        row_peak = lax.pmax(row_local, "col") * row_scale
        col_peak = lax.pmax(col_local, "row") * col_scale
        row_scale = row_scale / jnp.sqrt(row_peak + EPS)
        col_scale = col_scale / jnp.sqrt(col_peak + EPS)
    cost_scaled = col_scale * cost
    rhs_scaled = row_scale * rhs
    lower_scaled = lower / col_scale
    upper_scaled = upper / col_scale
    primal = primal_start / col_scale
    dual_vec = dual_start / row_scale
    first_row = (lax.axis_index("row") == 0).astype(jnp.float32)
    first_col = (lax.axis_index("col") == 0).astype(jnp.float32)
    cost_sq, rhs_sq = lax.psum(
        (
            jnp.sum(cost_scaled * cost_scaled) * first_row,
            jnp.sum(rhs_scaled * rhs_scaled) * first_col,
        ),
        ("row", "col"),
    )
    weight_ratio = jnp.sqrt(cost_sq + EPS) / jnp.sqrt(rhs_sq + EPS)
    step_size = step_start[0]

    def apply_matrix(vector):
        local_terms = forward_local(
            tiles, tile_rows, tile_cols, live_slots, col_scale * vector, row_blocks
        )
        return row_scale * lax.psum(local_terms, "col")

    image_now = apply_matrix(primal)
    for iteration in range(ITERS):
        pieces = (row_scale * dual_vec).reshape(row_blocks, tile_size)[tile_rows]
        product = jnp.einsum("sij,si->sj", tiles, pieces, precision=lax.Precision.HIGHEST)
        product = jnp.where(live_slots[:, None], product, 0.0)
        local_terms = (
            jnp.zeros((col_blocks, tile_size), jnp.float32).at[tile_cols].add(product).reshape(-1)
        )
        gradient = col_scale * lax.psum(local_terms, "row")
        primal_next = jnp.clip(
            primal - step_size / weight_ratio * (cost_scaled - gradient), lower_scaled, upper_scaled
        )
        image_next = apply_matrix(primal_next)
        dual_next = jnp.maximum(
            dual_vec + step_size * weight_ratio * (rhs_scaled - 2.0 * image_next + image_now), 0.0
        )
        primal_move = primal_next - primal
        dual_move = dual_next - dual_vec
        primal_sq = jnp.sum(primal_move * primal_move)
        dual_sq = jnp.sum(dual_move * dual_move)
        coupling = jnp.sum(dual_move * (image_next - image_now))
        primal_sq = lax.psum(primal_sq, "col")
        dual_sq, coupling = lax.psum((dual_sq, coupling), "row")
        movement = 0.5 * weight_ratio * primal_sq + 0.5 / weight_ratio * dual_sq + EPS
        growth = (1.0 + (iteration + 2.0) ** (-0.6)) * step_size
        limit_term = (1.0 - (iteration + 2.0) ** (-0.3)) * movement
        step_size = limit_term / jnp.maximum(jnp.abs(coupling), limit_term / growth)
        primal, dual_vec, image_now = (primal_next, dual_next, image_next)
    return (
        col_scale * primal,
        row_scale * dual_vec,
        row_scale,
        col_scale,
        jnp.reshape(step_size, (1,)),
    )


def solution(mesh):
    in_specs = (
        P(("grp", "row", "col"), None, None),
        P(("grp", "row", "col")),
        P(("grp", "row", "col")),
        P(("grp", "row", "col")),
        P(("grp", "col")),
        P(("grp", "col")),
        P(("grp", "col")),
        P(("grp", "row")),
        P(("grp", "col")),
        P(("grp", "row")),
        P("grp"),
    )
    out_specs = (
        P(("grp", "col")),
        P(("grp", "row")),
        P(("grp", "row")),
        P(("grp", "col")),
        P("grp"),
    )
    return jax.shard_map(body, mesh=mesh, in_specs=in_specs, out_specs=out_specs, check_vma=False)
```

profile of v0, /device:TPU:0, one launch (start us, length us, event | category | flops | bytes accessed | tf_op | source)
XLA Modules:
  0.0 505.8 jit_solution(10754492104799446386)
XLA Ops:
  7.2 0.0 all-reduce.14.cloned.1.call-start
  7.2 0.7 compare_select_fusion.1
  7.9 0.7 compare_select_fusion
  9.2 0.6 gather_fusion
  9.8 4.4 multiply_reduce_fusion.7
  14.3 1.6 scatter_custom_fusion
  15.9 0.0 all-reduce.22.cloned.1.call-start
  16.0 0.6 gather_fusion.1
  16.6 70.7 %all-reduce.14.cloned.1.call-done = f32[16384]{0:T(1024)} async-done(((f32[16384]{0:T(1024)}), f32[16384]{0:T(1024)}) %all-reduce.14.cloned.1.call-update) | async-done | bytes 65552 | tf_op jit(solution)/shard_map/pmax | solution.py:57
  87.3 0.9 fusion
  88.1 0.6 gather_fusion.3
  88.7 6.1 %multiply_reduce_fusion.4 = (f32[96,128]{1,0:T(8,128)S(1)}, f32[96,128]{1,0:T(8,128)S(1)}) fusion(f32[96,128,128]{2,1,0:T(8,128)} %param.11, f32[96,128]{1,0:T(8,128)S(1)} %gather_fusion.3, f32[96,128]{1,0:T(8,128)S(1)} %gather_fusion.1), kind=kLoop, calls=%fused_computation.30 | loop fusion | flops 7839744 | bytes 6488064 | tf_op jit(solution)/shard_map/reduce_max | solution.py:45
  94.9 1.0 scatter_custom_fusion.3
  95.9 1.0 scatter_custom_fusion.1
  96.8 3.3 all-reduce.7
  100.1 0.6 gather_fusion.4
  100.8 0.6 gather_fusion.2
  101.4 7.3 %multiply_reduce_fusion.3 = (f32[96,128]{1,0:T(8,128)S(1)}, f32[96,128]{1,0:T(8,128)S(1)}) fusion(f32[96,128,128]{2,1,0:T(8,128)} %param.11, f32[96,128]{1,0:T(8,128)S(1)} %gather_fusion.4, f32[96,128]{1,0:T(8,128)S(1)} %gather_fusion.2), kind=kLoop, calls=%fused_computation.29 | loop fusion | flops 7839744 | bytes 6488064 | tf_op jit(solution)/shard_map/reduce_max | solution.py:48
  108.7 1.6 scatter_custom_fusion.4
  110.2 1.6 scatter_custom_fusion.2
  111.8 0.0 all-reduce.16.cloned.1.call-start
  111.9 70.0 %all-reduce.22.cloned.1.call-done = (f32[16384]{0:T(1024)}, f32[16384]{0:T(1024)}) async-done(((f32[16384]{0:T(1024)}, f32[16384]{0:T(1024)}), (f32[16384]{0:T(1024)}, f32[16384]{0:T(1024)})) %all-reduce.22.cloned.1.call-update) | async-done | bytes 131088 | tf_op jit(solution)/shard_map/pmax | solution.py:57
  181.9 0.9 fusion.72
  182.8 0.6 gather_fusion.7
  183.5 0.6 gather_fusion.5
  184.1 6.1 %multiply_reduce_fusion = (f32[96,128]{1,0:T(8,128)S(1)}, f32[96,128]{1,0:T(8,128)S(1)}) fusion(f32[96,128,128]{2,1,0:T(8,128)} %param.11, f32[96,128]{1,0:T(8,128)S(1)} %gather_fusion.7, f32[96,128]{1,0:T(8,128)S(1)} %gather_fusion.5), kind=kLoop, calls=%fused_computation.26 | loop fusion | flops 7839744 | bytes 6488064 | tf_op jit(solution)/shard_map/reduce_max | solution.py:45
  190.2 1.1 scatter_custom_fusion.5
  191.4 1.0 scatter_custom_fusion.7
  192.3 3.3 all-reduce.6
  195.6 0.6 multiply_reduce_fusion.15
  196.3 0.6 gather_fusion.6
  197.0 4.5 multiply_reduce_fusion.1
  201.5 1.6 scatter_custom_fusion.6
  203.1 0.0 all-reduce.18.cloned.1.call-start
  203.2 0.6 gather_fusion.8
  203.8 7.3 %fusion.73 = f32[96,1,128]{2,1,0:T(1,128)S(1)} fusion(f32[96,128,1]{1,2,0:T(1,128)S(1)} %bitcast.89, f32[96,128,128]{2,1,0:T(8,128)} %param.11), kind=kOutput, calls=%fused_computation.136 | convolution fusion | flops 18874368 | bytes 6389760 | tf_op jit(solution)/shard_map/sij,si->sj/dot_general | solution.py:87
  211.1 1.6 scatter_custom_fusion.8
  212.7 0.0 all-reduce.18.cloned.1.call-update
  212.7 0.0 all-reduce.20.cloned.1.call-start
  213.4 57.7 %all-reduce.16.cloned.1.call-done = f32[16384]{0:T(1024)} async-done(((f32[16384]{0:T(1024)}), f32[16384]{0:T(1024)}) %all-reduce.16.cloned.1.call-update) | async-done | bytes 65552 | tf_op jit(solution)/shard_map/pmax | solution.py:57
  271.1 1.5 multiply_reduce_fusion.10
  273.9 30.9 %all-reduce = (f32[]{:T(128)}, f32[]{:T(128)}) all-reduce(f32[]{:T(128)S(6)} %mul.225, f32[]{:T(128)S(6)} %mul.231), channel_id=1, replica_groups=mesh['grp'=2,'row'=8,'col'=2] {'row','col'}, use_global_device_ids=true, to_apply=%region_22.23 | all-reduce | flops 2 | bytes 16 | tf_op jit(solution)/shard_map/psum | solution.py:68
  306.2 37.6 %all-reduce.18.cloned.1.call-done = f32[16384]{0:T(1024)} async-done(((f32[16384]{0:T(1024)}), f32[16384]{0:T(1024)}) %all-reduce.18.cloned.1.call-update) | async-done | bytes 65552 | tf_op jit(solution)/shard_map/psum | solution.py:92
  343.8 1.5 multiply_reduce_fusion.9
  345.3 0.6 gather_fusion.10
  345.9 11.8 %fusion.75 = f32[96,1,128]{2,1,0:T(1,128)S(1)} fusion(f32[96,128,1]{1,2,0:T(1,128)S(1)} %bitcast.90, f32[96,128,128]{2,1,0:T(8,128)} %param.11), kind=kOutput, calls=%fused_computation.138 | convolution fusion | flops 18874368 | bytes 6389760 | tf_op jit(solution)/shard_map/sij,sj->si/dot_general | solution.py:16
  357.7 1.2 scatter_custom_fusion.10
  358.9 0.6 gather_fusion.9
  359.6 11.8 %fusion.74 = f32[96,1,128]{2,1,0:T(1,128)S(1)} fusion(f32[96,128,1]{1,2,0:T(1,128)S(1)} %bitcast.91, f32[96,128,128]{2,1,0:T(8,128)} %param.11), kind=kOutput, calls=%fused_computation.137 | convolution fusion | flops 18874368 | bytes 6389760 | tf_op jit(solution)/shard_map/sij,sj->si/dot_general | solution.py:16
  371.4 1.0 scatter_custom_fusion.9
  372.4 4.5 all-reduce.5
  376.9 0.6 multiply_reduce_fusion.13
  377.5 0.6 gather_fusion.11
  378.2 7.3 %fusion.76 = f32[96,1,128]{2,1,0:T(1,128)S(1)} fusion(f32[96,128,1]{1,2,0:T(1,128)S(1)} %bitcast.88, f32[96,128,128]{2,1,0:T(8,128)} %param.11), kind=kOutput, calls=%fused_computation.139 | convolution fusion | flops 18874368 | bytes 6389760 | tf_op jit(solution)/shard_map/sij,si->sj/dot_general | solution.py:87
  385.5 1.6 scatter_custom_fusion.11
  387.1 20.9 %all-reduce.2 = (f32[]{:T(128)}, f32[]{:T(128)}) all-reduce(f32[]{:T(128)} %get-tuple-element.14, f32[]{:T(128)} %get-tuple-element.13), channel_id=1, replica_groups=mesh['grp'=2,'row'=8,'col'=2] {'row'}, use_global_device_ids=true, to_apply=%region_37.38 | all-reduce | flops 2 | bytes 16 | tf_op jit(solution)/shard_map/psum | solution.py:106
  410.1 45.7 %all-reduce.20.cloned.1.call-done = f32[16384]{0:T(1024)} async-done(((f32[16384]{0:T(1024)}), f32[16384]{0:T(1024)}) %all-reduce.20.cloned.1.call-update) | async-done | bytes 65552 | tf_op jit(solution)/shard_map/psum | solution.py:92
  455.7 1.5 multiply_reduce_fusion.8
  457.2 0.6 gather_fusion.12
  457.8 11.8 %fusion.77 = f32[96,1,128]{2,1,0:T(1,128)S(1)} fusion(f32[96,128,1]{1,2,0:T(1,128)S(1)} %bitcast.92, f32[96,128,128]{2,1,0:T(8,128)} %param.11), kind=kOutput, calls=%fused_computation.140 | convolution fusion | flops 18874368 | bytes 6389760 | tf_op jit(solution)/shard_map/sij,sj->si/dot_general | solution.py:16
  469.7 1.0 scatter_custom_fusion.12
  470.7 3.2 all-reduce.4
  474.5 1.3 multiply_reduce_fusion.11
  475.8 21.0 %all-reduce.1 = (f32[]{:T(128)}, f32[]{:T(128)}) all-reduce(f32[]{:T(128)} %get-tuple-element.12, f32[]{:T(128)} %get-tuple-element.11), channel_id=1, replica_groups=mesh['grp'=2,'row'=8,'col'=2] {'row'}, use_global_device_ids=true, to_apply=%region_47.48 | all-reduce | flops 2 | bytes 16 | tf_op jit(solution)/shard_map/psum | solution.py:106
  (38 shorter events, 0.2 us)
Async XLA Ops:
  7.2 80.1 %all-reduce.14.cloned.1.call-start = ((), (), s32[]{:S(2)}) async-start(), calls=%async_computation | async-start | bytes 131072 | tf_op jit(solution)/shard_map/pmax | solution.py:57
  15.9 166.0 %all-reduce.22.cloned.1.call-start = ((), (), s32[]{:S(2)}) async-start(), calls=%async_computation.4 | async-start | bytes 262144 | tf_op jit(solution)/shard_map/pmax | solution.py:57
  88.7 93.2 %copy-start.2 = (f32[16384]{0:T(1024)S(1)}, f32[16384]{0:T(1024)}, u32[]{:S(2)}) copy-start(f32[16384]{0:T(1024)} %all-reduce.14.cloned.1.call-done) | copy-start | bytes 196612
  101.4 94.2 %copy-start.11 = (f32[2048]{0:T(1024)S(1)}, f32[2048]{0:T(1024)}, u32[]{:S(2)}) copy-start(f32[2048]{0:T(1024)} %param.18) | copy-start | bytes 24580
  111.8 159.3 %all-reduce.16.cloned.1.call-start = ((), (), s32[]{:S(2)}) async-start(), calls=%async_computation.1 | async-start | bytes 131072 | tf_op jit(solution)/shard_map/pmax | solution.py:57
  184.1 19.1 %copy-start.10 = (f32[2048]{0:T(1024)S(1)}, f32[2048]{0:T(1024)}, u32[]{:S(2)}) copy-start(f32[2048]{0:T(1024)} %param.20) | copy-start | bytes 24580
  196.3 278.2 %copy-start.5 = (f32[2048]{0:T(1024)}, f32[2048]{0:T(1024)S(1)}, u32[]{:S(2)}) copy-start(f32[2048]{0:T(1024)S(1)} %get-tuple-element.42) | copy-start | bytes 24580
  196.9 74.2 %copy-start.3 = (f32[16384]{0:T(1024)S(1)}, f32[16384]{0:T(1024)}, u32[]{:S(2)}) copy-start(f32[16384]{0:T(1024)} %get-tuple-element.21) | copy-start | bytes 196612
  196.9 74.2 %copy-start.4 = (f32[16384]{0:T(1024)S(1)}, f32[16384]{0:T(1024)}, u32[]{:S(2)}) copy-start(f32[16384]{0:T(1024)} %get-tuple-element.22) | copy-start | bytes 196612
  196.9 74.2 %copy-start.9 = (f32[16384]{0:T(1024)S(1)}, f32[16384]{0:T(1024)}, u32[]{:S(2)}) copy-start(f32[16384]{0:T(1024)} %param.15) | copy-start | bytes 196612
  196.9 146.8 %copy-start.6 = (f32[16384]{0:T(1024)S(1)}, f32[16384]{0:T(1024)}, u32[]{:S(2)}) copy-start(f32[16384]{0:T(1024)} %param.19) | copy-start | bytes 196612
  196.9 146.8 %copy-start.7 = (f32[16384]{0:T(1024)S(1)}, f32[16384]{0:T(1024)}, u32[]{:S(2)}) copy-start(f32[16384]{0:T(1024)} %param.16) | copy-start | bytes 196612
  196.9 146.8 %copy-start.8 = (f32[16384]{0:T(1024)S(1)}, f32[16384]{0:T(1024)}, u32[]{:S(2)}) copy-start(f32[16384]{0:T(1024)} %param.17) | copy-start | bytes 196612
  203.1 140.6 %all-reduce.18.cloned.1.call-start = ((), (), s32[]{:S(2)}) async-start(), calls=%async_computation.2 | async-start | bytes 131072 | tf_op jit(solution)/shard_map/psum | solution.py:92
  212.7 243.0 %all-reduce.20.cloned.1.call-start = ((), (), s32[]{:S(2)}) async-start(), calls=%async_computation.3 | async-start | bytes 131072 | tf_op jit(solution)/shard_map/psum | solution.py:92
  272.6 184.6 %copy-start.1 = (f32[16384]{0:T(1024)}, f32[16384]{0:T(1024)S(1)}, u32[]{:S(2)}) copy-start(f32[16384]{0:T(1024)S(1)} %get-tuple-element.45) | copy-start | bytes 196612
  457.2 40.9 %copy-start = (f32[16384]{0:T(1024)}, f32[16384]{0:T(1024)S(1)}, u32[]{:S(2)}) copy-start(f32[16384]{0:T(1024)S(1)} %mul.254) | copy-start | bytes 196612
Sparse Core Ops, SparseCore 0:
  16.0 71.2 all-reduce.13
  112.0 69.9 all-reduce.21
  203.2 67.8 all-reduce.15
  275.3 68.3 all-reduce.17
  387.2 68.4 all-reduce.19
where the time goes:
time: 507 us; the launch traced here: 506 us
  waiting for transfers between devices  282 us (56%)
  blocking collectives  87 us (17%)
  other arithmetic  55.3 us (11%)
  matrix products  50.2 us (10%)
  between operations  23.1 us (5%)
  local copies, waits for them, and re-layouts  8.15 us (2%)
    pmax x3, waiting for transfers between devices, body(): col_peak = lax.pmax(col_local, 'row') * col_scale  198 us
    psum x2, waiting for transfers between devices, body(): gradient = col_scale * lax.psum(local_terms, 'row')  83.2 us
    psum x2, blocking collectives, body(): dual_sq, coupling = lax.psum((dual_sq, coupling), 'row')  41.9 us
    dot_general x3, matrix products, forward_local(): jnp.einsum('sij,sj->si', tiles, pieces, precision=lax.Precision.HIGHEST)  35.5 us
    psum x1, blocking collectives, body(): lax.psum((jnp.sum(cost_scaled * cost_scaled) * first_row, jnp.sum(rhs_sca...  30.9 us
    reduce_max x3, other arithmetic, body(): jnp.max(magnitude * row_pieces[:, :, None], axis=1)  16.3 us
    dot_general x2, matrix products, body(): jnp.einsum('sij,si->sj', tiles, pieces, precision=lax.Precision.HIGHEST)  14.6 us
    reduce_max x2, other arithmetic, body(): jnp.max(magnitude * col_pieces[:, None, :], axis=2)  12.3 us
  transfers between devices with their start and end apart: 5, of which 5 were waited for; matrix products, arithmetic and copies ran while one was open for 2% of the time, Pallas kernels for 0%

commit v1 on v0

v1 whole, which is shorter than its diff:
```python
import functools

import jax
import jax.numpy as jnp
from jax import lax
from jax.experimental import pallas as pl
from jax.experimental.pallas import tpu as pltpu
from jax.sharding import PartitionSpec as P

RUIZ = 4
ITERS = 2
EPS = 1e-06
MESH = pl.DeviceIdType.MESH
SIDE = 8


def kernel(
    n_row,
    n_col,
    tr_ref,
    tc_ref,
    count_ref,
    step_ref,
    tiles_ref,
    cost_ref,
    lower_ref,
    upper_ref,
    rhs_ref,
    primal_ref,
    dual_ref,
    primal_out,
    dual_out,
    rscale_out,
    cscale_out,
    step_out,
    rowmat,
    colvec,
    colpart,
    rowpart,
    rs_send,
    rs_recv,
    ag_recv,
    pair_recv,
    last_recv,
    rs_ssem,
    rs_rsem,
    ag_ssem,
    ag_rsem,
    pair_ssem,
    pair_rsem,
    last_ssem,
    last_rsem,
):
    slots, tile, _ = tiles_ref.shape
    row_blocks = rhs_ref.shape[0]
    col_blocks = cost_ref.shape[0]
    own = col_blocks // n_row
    unroll = next(u for u in (8, 4, 2, 1) if slots % u == 0)
    grp = lax.axis_index("grp")
    me = lax.axis_index("row")
    core = lax.axis_index("col")
    mine = pl.ds(pl.multiple_of(me * own, own), own)
    count = count_ref[0]

    barrier = pltpu.get_barrier_semaphore()

    def greet(step, _):
        peer = lax.rem(me + step, n_row)
        pl.semaphore_signal(barrier, inc=1, device_id=(grp, peer, core), device_id_type=MESH)
        return 0

    lax.fori_loop(1, n_row, greet, 0)
    for step in range(1, n_col):
        peer = lax.rem(core + step, n_col)
        pl.semaphore_signal(barrier, inc=1, device_id=(grp, me, peer), device_id_type=MESH)

    def over_peers(act):
        def body(step, _):
            act(lax.rem(me + step, n_row))
            return 0

        lax.fori_loop(1, n_row, body, 0)

    def rs_copy(k, peer, source):
        return pltpu.make_async_remote_copy(
            src_ref=rs_send.at[k, peer],
            dst_ref=rs_recv.at[k, source],
            send_sem=rs_ssem.at[k, peer],
            recv_sem=rs_rsem.at[k, source],
            device_id=(grp, peer, core),
            device_id_type=MESH,
        )

    def ag_copy(k, peer, source):
        return pltpu.make_async_remote_copy(
            src_ref=ag_recv.at[k, source],
            dst_ref=ag_recv.at[k, source],
            send_sem=ag_ssem.at[k, peer],
            recv_sem=ag_rsem.at[k, source],
            device_id=(grp, peer, core),
            device_id_type=MESH,
        )

    def last_copy(peer, source):
        return pltpu.make_async_remote_copy(
            src_ref=last_recv.at[source],
            dst_ref=last_recv.at[source],
            send_sem=last_ssem.at[peer],
            recv_sem=last_rsem.at[source],
            device_id=(grp, peer, core),
            device_id_type=MESH,
        )

    def pair_copy(k, peer, source):
        return pltpu.make_async_remote_copy(
            src_ref=pair_recv.at[k, source],
            dst_ref=pair_recv.at[k, source],
            send_sem=pair_ssem.at[k, peer],
            recv_sem=pair_rsem.at[k, source],
            device_id=(grp, me, peer),
            device_id_type=MESH,
        )

    def send_pair(k, value, side):
        pair_recv[k, core, 0:row_blocks] = value
        pair_recv[k, core, row_blocks : row_blocks + SIDE] = jnp.broadcast_to(side, (SIDE, tile))
        for step in range(1, n_col):
            pair_copy(k, lax.rem(core + step, n_col), core).start()

    def take_pair(k, combine):
        for step in range(1, n_col):
            peer = lax.rem(core + step, n_col)
            pair_copy(k, peer, peer).wait_recv()
        value = pair_recv[k, 0, 0:row_blocks]
        side = pair_recv[k, 0, row_blocks : row_blocks + SIDE]
        for c in range(1, n_col):
            value = combine(value, pair_recv[k, c, 0:row_blocks])
            side = side + pair_recv[k, c, row_blocks : row_blocks + SIDE]
        return value, side

    def scatter_cols(k, combine, side):
        ids = lax.broadcasted_iota(jnp.int32, (own, tile), 0)

        def owner(p, _):
            first = p * own

            def group(i, total):
                for u in range(unroll):
                    s = i * unroll + u
                    at = jnp.where(s < count, tc_ref[s] - first, -1)
                    part = colpart[pl.ds(s, 1), :]
                    total = combine(total, jnp.where(ids == at, part, 0.0))
                return total

            total = lax.fori_loop(
                0, slots // unroll, group, jnp.zeros((own, tile), jnp.float32)
            )
            rs_send[k, p, 0:own] = total
            rs_send[k, p, own : own + SIDE] = jnp.broadcast_to(side, (SIDE, tile))
            return 0

        lax.fori_loop(0, n_row, owner, 0)
        rs_recv[k, me] = rs_send[k, me]

    def send_rs(k):
        over_peers(lambda peer: rs_copy(k, peer, me).start())

    def take_rs(k, combine):
        over_peers(lambda peer: rs_copy(k, peer, peer).wait_recv())
        value = rs_recv[k, 0, 0:own]
        side = rs_recv[k, 0, own : own + SIDE]
        for p in range(1, n_row):
            value = combine(value, rs_recv[k, p, 0:own])
            side = side + rs_recv[k, p, own : own + SIDE]
        return value, side

    def send_ag(k, value, side):
        ag_recv[k, me, 0:own] = value
        ag_recv[k, me, own : own + SIDE] = jnp.broadcast_to(side, (SIDE, tile))
        over_peers(lambda peer: ag_copy(k, peer, me).start())

    def take_ag(k):
        over_peers(lambda peer: ag_copy(k, peer, peer).wait_recv())
        side = ag_recv[k, 0, own : own + SIDE]
        for p in range(n_row):
            colvec[p * own : (p + 1) * own, :] = ag_recv[k, p, 0:own]
            if p > 0:
                side = side + ag_recv[k, p, own : own + SIDE]
        return side

    def set_rows(vector):
        for r in range(row_blocks):
            wide = jnp.broadcast_to(vector[r : r + 1, :], (tile, tile))
            rowmat[r] = jnp.transpose(wide)

    def col_pass(reduce, transform):
        def group(i, _):
            for u in range(unroll):
                s = i * unroll + u
                block = transform(tiles_ref[s] * rowmat[tr_ref[s]])
                colpart[pl.ds(s, 1), :] = reduce(block, axis=0, keepdims=True)
            return 0

        lax.fori_loop(0, slots // unroll, group, 0)

    def row_pass(reduce, transform, combine):
        lanes = lax.broadcasted_iota(jnp.int32, (tile, tile), 1)

        def group(i, total):
            for u in range(unroll):
                s = i * unroll + u
                block = transform(tiles_ref[s] * colvec[pl.ds(tc_ref[s], 1), :])
                total = jnp.where(lanes == s, reduce(block, axis=1, keepdims=True), total)
            return total

        total = lax.fori_loop(
            0, slots // unroll, group, jnp.zeros((tile, tile), jnp.float32)
        )
        rowpart[...] = jnp.transpose(total)
        ids = lax.broadcasted_iota(jnp.int32, (row_blocks, tile), 0)

        def place(i, total):
            for u in range(unroll):
                s = i * unroll + u
                at = jnp.where(s < count, tr_ref[s], -1)
                part = rowpart[pl.ds(s, 1), :]
                total = combine(total, jnp.where(ids == at, part, 0.0))
            return total

        return lax.fori_loop(
            0, slots // unroll, place, jnp.zeros((row_blocks, tile), jnp.float32)
        )

    def plain(block):
        return block

    add = jnp.add
    none = jnp.zeros((1, tile), jnp.float32)

    def total_of(value):
        part = jnp.sum(jnp.sum(value, axis=0, keepdims=True), axis=1, keepdims=True)
        return jnp.broadcast_to(part, (1, tile))

    row_scale = jnp.ones((row_blocks, tile), jnp.float32)
    col_scale = jnp.ones((own, tile), jnp.float32)
    colvec[...] = jnp.ones((col_blocks, tile), jnp.float32)
    for sweep in range(RUIZ):
        set_rows(row_scale)
        col_pass(jnp.max, jnp.abs)
        scatter_cols(sweep, jnp.maximum, none)
        if sweep == 0:
            pl.semaphore_wait(barrier, n_row + n_col - 2)
        send_rs(sweep)
        if sweep > 0:
            take_ag(sweep - 1)
        row_local = row_pass(jnp.max, jnp.abs, jnp.maximum)
        send_pair(sweep, row_local, none)
        col_peak = take_rs(sweep, jnp.maximum)[0] * col_scale
        col_scale = col_scale / jnp.sqrt(col_peak + EPS)
        send_ag(sweep, col_scale, none)
        row_peak = take_pair(sweep, jnp.maximum)[0] * row_scale
        row_scale = row_scale / jnp.sqrt(row_peak + EPS)

    rscale_out[...] = row_scale
    rhs_scaled = row_scale * rhs_ref[...]
    dual = dual_ref[...] / row_scale
    set_rows(row_scale * dual)
    col_pass(jnp.sum, plain)
    scatter_cols(RUIZ, add, total_of(rhs_scaled * rhs_scaled))
    send_rs(RUIZ)

    take_ag(RUIZ - 1)
    whole_scale = colvec[...]
    cscale_out[...] = whole_scale
    whole_cost = whole_scale * cost_ref[...]
    colvec[...] = whole_scale * (primal_ref[...] / whole_scale)
    send_pair(RUIZ, row_pass(jnp.sum, plain, add), total_of(whole_cost * whole_cost))

    cost_scaled = col_scale * cost_ref[mine, :]
    lower_scaled = lower_ref[mine, :] / col_scale
    upper_scaled = upper_ref[mine, :] / col_scale
    primal = primal_ref[mine, :] / col_scale
    eta = jnp.full((1, tile), step_ref[0], jnp.float32)

    side_rows = lax.broadcasted_iota(jnp.int32, (SIDE, tile), 0)
    weight = None
    image = None
    before = None
    for k in range(ITERS):
        gradient, side = take_rs(RUIZ + k, add)
        gradient = col_scale * gradient
        if k == 0:
            image, cost_side = take_pair(RUIZ, add)
            image = row_scale * image
            weight = jnp.sqrt(cost_side[0:1] + EPS) / jnp.sqrt(side[0:1] + EPS)
        else:
            eta = next_step(k - 1, eta, weight, before, side)
        primal_next = jnp.clip(
            primal - eta / weight * (cost_scaled - gradient), lower_scaled, upper_scaled
        )
        moved = primal_next - primal
        send_ag(RUIZ + k, col_scale * primal_next, total_of(moved * moved))
        primal = primal_next
        moved_sq = take_ag(RUIZ + k)[0:1]
        send_pair(RUIZ + 1 + k, row_pass(jnp.sum, plain, add), moved_sq)
        image_next, before = take_pair(RUIZ + 1 + k, add)
        before = before[0:1]
        image_next = row_scale * image_next
        dual_next = jnp.maximum(
            dual + eta * weight * (rhs_scaled - 2.0 * image_next + image), 0.0
        )
        moved = dual_next - dual
        both = jnp.where(
            side_rows == 0,
            total_of(moved * moved),
            total_of(moved * (image_next - image)),
        )
        dual, image = dual_next, image_next
        if k < ITERS - 1:
            set_rows(row_scale * dual)
            col_pass(jnp.sum, plain)
            scatter_cols(RUIZ + 1 + k, add, both)
            send_rs(RUIZ + 1 + k)
        else:
            last_recv[me] = both
            over_peers(lambda peer: last_copy(peer, me).start())
            primal_out[...] = colvec[...]
            dual_out[...] = row_scale * dual
            over_peers(lambda peer: last_copy(peer, peer).wait_recv())
            side = last_recv[0]
            for p in range(1, n_row):
                side = side + last_recv[p]
            eta = next_step(k, eta, weight, before, side)
    step_out[...] = eta[:, 0:1]

    for k in range(RUIZ + ITERS):
        over_peers(lambda peer: rs_copy(k, peer, me).wait_send())
        over_peers(lambda peer: ag_copy(k, peer, me).wait_send())
    for k in range(RUIZ + ITERS + 1):
        for step in range(1, n_col):
            pair_copy(k, lax.rem(core + step, n_col), core).wait_send()
    over_peers(lambda peer: last_copy(peer, me).wait_send())


def next_step(k, eta, weight, primal_sq, side):
    dual_sq, coupling = side[0:1], side[1:2]
    movement = 0.5 * weight * primal_sq + 0.5 / weight * dual_sq + EPS
    growth = (1.0 + (k + 2.0) ** (-0.6)) * eta
    limit = (1.0 - (k + 2.0) ** (-0.3)) * movement
    return limit / jnp.maximum(jnp.abs(coupling), limit / growth)


def body(
    n_row,
    n_col,
    tiles,
    tile_rows,
    tile_cols,
    counts,
    cost,
    lower,
    upper,
    rhs,
    primal_start,
    dual_start,
    step_start,
):
    slots, tile, _ = tiles.shape
    row_blocks = rhs.shape[0] // tile
    col_blocks = cost.shape[0] // tile
    own = col_blocks // n_row
    phases = RUIZ + ITERS
    smem = pl.BlockSpec(memory_space=pltpu.SMEM)
    vmem = pl.BlockSpec(memory_space=pltpu.VMEM)
    f32 = jnp.float32

    def cols(x):
        return x.reshape(col_blocks, tile)

    def rows(x):
        return x.reshape(row_blocks, tile)

    dma = pltpu.SemaphoreType.DMA
    primal, dual, row_scale, col_scale, step = pl.pallas_call(
        functools.partial(kernel, n_row, n_col),
        out_shape=(
            jax.ShapeDtypeStruct((col_blocks, tile), f32),
            jax.ShapeDtypeStruct((row_blocks, tile), f32),
            jax.ShapeDtypeStruct((row_blocks, tile), f32),
            jax.ShapeDtypeStruct((col_blocks, tile), f32),
            jax.ShapeDtypeStruct((1, 1), f32),
        ),
        in_specs=[smem] * 4 + [vmem] * 7,
        out_specs=(vmem,) * 5,
        scratch_shapes=[
            pltpu.VMEM((row_blocks, tile, tile), f32),
            pltpu.VMEM((col_blocks, tile), f32),
            pltpu.VMEM((slots, tile), f32),
            pltpu.VMEM((tile, tile), f32),
            pltpu.VMEM((phases, n_row, own + SIDE, tile), f32),
            pltpu.VMEM((phases, n_row, own + SIDE, tile), f32),
            pltpu.VMEM((phases, n_row, own + SIDE, tile), f32),
            pltpu.VMEM((phases + 1, n_col, row_blocks + SIDE, tile), f32),
            pltpu.VMEM((n_row, SIDE, tile), f32),
            dma((phases, n_row)),
            dma((phases, n_row)),
            dma((phases, n_row)),
            dma((phases, n_row)),
            dma((phases + 1, n_col)),
            dma((phases + 1, n_col)),
            dma((n_row,)),
            dma((n_row,)),
        ],
        compiler_params=pltpu.CompilerParams(
            collective_id=0, has_side_effects=True, vmem_limit_bytes=40 * 1024 * 1024
        ),
        name="equilibrate_and_iterate",
    )(
        tile_rows,
        tile_cols,
        counts,
        step_start,
        tiles,
        cols(cost),
        cols(lower),
        cols(upper),
        rows(rhs),
        cols(primal_start),
        rows(dual_start),
    )
    return (
        primal.reshape(-1),
        dual.reshape(-1),
        row_scale.reshape(-1),
        col_scale.reshape(-1),
        step.reshape(-1),
    )


def solution(mesh):
    in_specs = (
        P(("grp", "row", "col"), None, None),
        P(("grp", "row", "col")),
        P(("grp", "row", "col")),
        P(("grp", "row", "col")),
        P(("grp", "col")),
        P(("grp", "col")),
        P(("grp", "col")),
        P(("grp", "row")),
        P(("grp", "col")),
        P(("grp", "row")),
        P("grp"),
    )
    out_specs = (
        P(("grp", "col")),
        P(("grp", "row")),
        P(("grp", "row")),
        P(("grp", "col")),
        P("grp"),
    )
    local = functools.partial(body, mesh.shape["row"], mesh.shape["col"])
    return jax.shard_map(local, mesh=mesh, in_specs=in_specs, out_specs=out_specs, check_vma=False)
```

time: 507 us -> 88.8 us (0.18)
  waiting for transfers between devices: 282 us -> 0 us
  blocking collectives: 87 us -> 0 us
  Pallas kernels: 0 us -> 73.3 us
  other arithmetic: 55.3 us -> 0 us
  matrix products: 50.2 us -> 0 us
  between operations: 23.1 us -> 3.71 us
    pmax x3 -> x0, waiting for transfers between devices: 198 us -> none  [body(): col_peak = lax.pmax(col_local, 'row') * col_scale]
    psum x2 -> x0, waiting for transfers between devices: 83.2 us -> none  [body(): gradient = col_scale * lax.psum(local_terms, 'row')]
    psum x5 -> x0, blocking collectives: 80.5 us -> none  [the longest x2 41.9 us: body(): dual_sq, coupling = lax.psum((dual_sq, coupling), 'row')]
    pallas_call x0 -> x1, Pallas kernels: none -> 73.3 us  [body(): pl.pallas_call(functools.partial(kernel, n_row, n_col), out_shape=(jax.Sh...]
    dot_general x5 -> x0, matrix products: 50.2 us -> none  [the longest x3 35.5 us: forward_local(): jnp.einsum('sij,sj->si', tiles, pieces, precision=lax.Precision.HIGHEST)]
    reduce_max x5 -> x0, other arithmetic: 28.5 us -> none  [the longest x3 16.3 us: body(): jnp.max(magnitude * row_pieces[:, :, None], axis=1)]
    unnamed x24 -> x22, local copies, waits for them, and re-layouts: 0.06 us -> 11.3 us
    another operation x8 -> x0, other arithmetic: 10.3 us -> none  [the longest x4 6.27 us: body(): jnp.zeros((col_blocks, tile_size), jnp.float32).at[tile_cols].max(col_part)]
  transfers between devices with their start and end apart: 5 -> 0, of which waited for: 5 -> 0; matrix products, arithmetic and copies ran while one was open for 2% -> 0% of each run, Pallas kernels for 0% -> 0%
where the time goes in v1:
time: 88.8 us; the launch traced here: 88.3 us
  Pallas kernels  73.3 us (83%)
  local copies, waits for them, and re-layouts  11.3 us (13%)
  between operations  3.71 us (4%)
    pallas_call x1, Pallas kernels, body(): pl.pallas_call(functools.partial(kernel, n_row, n_col), out_shape=(jax.Sh...  73.3 us
    unnamed x22, local copies, waits for them, and re-layouts  11.3 us

profile of v1, /device:TPU:0, one launch (start us, length us, event | category | flops | bytes accessed | tf_op | source)
XLA Modules:
  0.0 88.3 jit_solution(7748069820644104737)
XLA Ops:
  1.9 0.0 copy-start
  1.9 2.8 %copy-done = f32[96,128,128]{2,1,0:T(8,128)S(1)} copy-done((f32[96,128,128]{2,1,0:T(8,128)S(1)}, f32[96,128,128]{2,1,0:T(8,128)}, u32[]{:S(2)}) %copy-start) | copy-done | bytes 6291480
  4.7 0.0 copy-start.1
  4.7 0.8 copy-done.1
  5.6 0.0 copy-start.2
  5.6 0.8 copy-done.2
  6.4 0.0 copy-start.3
  6.4 0.8 copy-done.3
  7.2 0.0 copy-start.4
  7.2 0.8 copy-done.4
  8.1 0.0 copy-start.5
  8.1 0.7 copy-done.5
  8.8 0.0 copy-start.6
  8.8 0.7 copy-done.6
  9.5 0.0 copy-start.7
  9.5 0.7 copy-done.7
  10.1 0.0 copy-start.8
  10.1 0.7 copy-done.8
  10.8 73.3 %equilibrate_and_iterate.1 = (f32[128,128]{1,0:T(8,128)S(1)}, f32[16,128]{1,0:T(8,128)S(1)}, f32[16,128]{1,0:T(8,128)S(1)}, f32[128,128]{1,0:T(8,128)S(1)}, f32[1,1]{1,0:T(1,128)}) custom-call(s32[96]{0:T(128)S(1)} %copy-done.7, s32[96]{0:T(128)S(1)} %copy-done.8, s32[1]{0:T(128)S(6)} %copy.21.count_ref, f32[1]{0:T(128)S(6)} %copy.22.step_ref, ...), custom_call_target="tpu_custom_call" | custom-call | tf_op jit(solution)/shard_map/equilibrate_and_iterate/pallas_call | solution.py:384
  84.1 0.6 copy.23
  84.7 0.6 copy.24
  85.3 0.6 copy.25
  85.9 0.6 copy.26
Async XLA Ops:
  1.9 2.8 %copy-start = (f32[96,128,128]{2,1,0:T(8,128)S(1)}, f32[96,128,128]{2,1,0:T(8,128)}, u32[]{:S(2)}) copy-start(f32[96,128,128]{2,1,0:T(8,128)} %tiles_ref.1) | copy-start | bytes 18874372
  4.7 0.8 copy-start.1
  5.6 0.8 copy-start.2
  6.4 0.8 copy-start.3
  7.2 0.8 copy-start.4
  8.1 0.7 copy-start.5
  8.8 0.7 copy-start.6
  9.5 0.7 copy-start.7
  10.1 0.7 copy-start.8

commit v2 on v1

--- a/solution.py
+++ b/solution.py
@@ -17,10 +17,24 @@
 def kernel(
     n_row,
     n_col,
+    count_ref,
+    step_ref,
+    tr_hbm,
+    tc_hbm,
+    tiles_hbm,
+    cost_hbm,
+    lower_hbm,
+    upper_hbm,
+    rhs_hbm,
+    primal_hbm,
+    dual_hbm,
+    primal_out,
+    dual_out,
+    rscale_out,
+    cscale_out,
+    step_out,
     tr_ref,
     tc_ref,
-    count_ref,
-    step_ref,
     tiles_ref,
     cost_ref,
     lower_ref,
@@ -28,15 +42,16 @@
     rhs_ref,
     primal_ref,
     dual_ref,
-    primal_out,
-    dual_out,
-    rscale_out,
-    cscale_out,
-    step_out,
+    load_sem,
+    tile_sem,
+    listed,
+    order,
+    order_sem,
+    keycol,
+    running,
     rowmat,
     colvec,
     colpart,
-    rowpart,
     rs_send,
     rs_recv,
     ag_recv,
@@ -62,6 +77,36 @@
     mine = pl.ds(pl.multiple_of(me * own, own), own)
     count = count_ref[0]
 
+    small = [
+        pltpu.make_async_copy(source, target, load_sem.at[i])
+        for i, (source, target) in enumerate(
+            [
+                (tr_hbm, tr_ref),
+                (tc_hbm, tc_ref),
+                (cost_hbm, cost_ref),
+                (lower_hbm, lower_ref),
+                (upper_hbm, upper_ref),
+                (rhs_hbm, rhs_ref),
+                (primal_hbm, primal_ref),
+                (dual_hbm, dual_ref),
+            ]
+        )
+    ]
+
+    def tile_copy(i):
+        some = pl.ds(i * unroll, unroll)
+        return pltpu.make_async_copy(tiles_hbm.at[some], tiles_ref.at[some], tile_sem.at[i])
+
+    def load_tiles(i, _):
+        tile_copy(i).start()
+        return 0
+
+    small[0].start()
+    small[1].start()
+    lax.fori_loop(0, slots // unroll, load_tiles, 0)
+    for copy in small[2:]:
+        copy.start()
+
     barrier = pltpu.get_barrier_semaphore()
 
     def greet(step, _):
@@ -81,10 +126,13 @@
 
         lax.fori_loop(1, n_row, body, 0)
 
+    def length(k):
+        return own if k < RUIZ else own + SIDE
+
     def rs_copy(k, peer, source):
         return pltpu.make_async_remote_copy(
-            src_ref=rs_send.at[k, peer],
-            dst_ref=rs_recv.at[k, source],
+            src_ref=rs_send.at[k, peer, pl.ds(0, length(k))],
+            dst_ref=rs_recv.at[k, source, pl.ds(0, length(k))],
             send_sem=rs_ssem.at[k, peer],
             recv_sem=rs_rsem.at[k, source],
             device_id=(grp, peer, core),
@@ -93,8 +141,8 @@
 
     def ag_copy(k, peer, source):
         return pltpu.make_async_remote_copy(
-            src_ref=ag_recv.at[k, source],
-            dst_ref=ag_recv.at[k, source],
+            src_ref=ag_recv.at[k, source, pl.ds(0, length(k))],
+            dst_ref=ag_recv.at[k, source, pl.ds(0, length(k))],
             send_sem=ag_ssem.at[k, peer],
             recv_sem=ag_rsem.at[k, source],
             device_id=(grp, peer, core),
@@ -139,10 +187,11 @@
         return value, side
 
     def scatter_cols(k, combine, side):
-        ids = lax.broadcasted_iota(jnp.int32, (own, tile), 0)
-
-        def owner(p, _):
-            first = p * own
+        owners = next(p for p in (4, 2, 1) if n_row % p == 0)
+        ids = lax.broadcasted_iota(jnp.int32, (owners * own, tile), 0)
+
+        def some(p, _):
+            first = p * (owners * own)
 
             def group(i, total):
                 for u in range(unroll):
@@ -153,14 +202,18 @@
                 return total
 
             total = lax.fori_loop(
-                0, slots // unroll, group, jnp.zeros((own, tile), jnp.float32)
+                0, slots // unroll, group, jnp.zeros((owners * own, tile), jnp.float32)
             )
-            rs_send[k, p, 0:own] = total
-            rs_send[k, p, own : own + SIDE] = jnp.broadcast_to(side, (SIDE, tile))
+            for q in range(owners):
+                rs_send[k, p * owners + q, 0:own] = total[q * own : (q + 1) * own]
+                if k >= RUIZ:
+                    rs_send[k, p * owners + q, own : own + SIDE] = jnp.broadcast_to(
+                        side, (SIDE, tile)
+                    )
             return 0
 
-        lax.fori_loop(0, n_row, owner, 0)
-        rs_recv[k, me] = rs_send[k, me]
+        lax.fori_loop(0, n_row // owners, some, 0)
+        rs_recv[k, me, 0 : length(k)] = rs_send[k, me, 0 : length(k)]
 
     def send_rs(k):
         over_peers(lambda peer: rs_copy(k, peer, me).start())
@@ -168,24 +221,30 @@
     def take_rs(k, combine):
         over_peers(lambda peer: rs_copy(k, peer, peer).wait_recv())
         value = rs_recv[k, 0, 0:own]
+        for p in range(1, n_row):
+            value = combine(value, rs_recv[k, p, 0:own])
+        if k < RUIZ:
+            return value, None
         side = rs_recv[k, 0, own : own + SIDE]
         for p in range(1, n_row):
-            value = combine(value, rs_recv[k, p, 0:own])
             side = side + rs_recv[k, p, own : own + SIDE]
         return value, side
 
     def send_ag(k, value, side):
         ag_recv[k, me, 0:own] = value
-        ag_recv[k, me, own : own + SIDE] = jnp.broadcast_to(side, (SIDE, tile))
+        if k >= RUIZ:
+            ag_recv[k, me, own : own + SIDE] = jnp.broadcast_to(side, (SIDE, tile))
         over_peers(lambda peer: ag_copy(k, peer, me).start())
 
     def take_ag(k):
         over_peers(lambda peer: ag_copy(k, peer, peer).wait_recv())
-        side = ag_recv[k, 0, own : own + SIDE]
         for p in range(n_row):
             colvec[p * own : (p + 1) * own, :] = ag_recv[k, p, 0:own]
-            if p > 0:
-                side = side + ag_recv[k, p, own : own + SIDE]
+        if k < RUIZ:
+            return None
+        side = ag_recv[k, 0, own : own + SIDE]
+        for p in range(1, n_row):
+            side = side + ag_recv[k, p, own : own + SIDE]
         return side
 
     def set_rows(vector):
@@ -193,43 +252,71 @@
             wide = jnp.broadcast_to(vector[r : r + 1, :], (tile, tile))
             rowmat[r] = jnp.transpose(wide)
 
-    def col_pass(reduce, transform):
+    def sort_slots():
+        subs = lax.broadcasted_iota(jnp.int32, (tile, tile), 0)
+        lanes = lax.broadcasted_iota(jnp.int32, (tile, tile), 1)
+        lane = lax.broadcasted_iota(jnp.int32, (1, tile), 1)
+        far = row_blocks + 1
+        keycol[0] = jnp.full((tile, tile), far, jnp.int32)
+        keys = jnp.full((1, tile), far, jnp.int32)
+        for s in range(slots):
+            key = jnp.where(s < count, tr_ref[s], row_blocks)
+            keycol[0, s : s + 1, :] = jnp.full((1, tile), key, jnp.int32)
+            keys = jnp.where(lane == s, key, keys)
+        col = keycol[0]
+        ahead = (col < keys) | ((col == keys) & (subs < lanes))
+        listed[0, 0:1, :] = jnp.sum(ahead.astype(jnp.int32), axis=0, keepdims=True)
+        copy = pltpu.make_async_copy(listed.at[0], order.at[0], order_sem.at[0])
+        copy.start()
+        until = jnp.sum((col <= lanes).astype(jnp.int32), axis=0, keepdims=True)
+        held = jnp.sum((col == lanes).astype(jnp.int32), axis=0, keepdims=True)
+        listed[1, 2:3, :] = jnp.where(held > 0, until - 1, slots)
+        copy.wait()
+        keycol[1] = jnp.full((tile, tile), 2 * tile, jnp.int32)
+        for s in range(slots):
+            keycol[1, s : s + 1, :] = jnp.full((1, tile), order[0, 0, s], jnp.int32)
+        rank = keycol[1]
+        here = jnp.sum(jnp.where(rank == lanes, col, 0), axis=0, keepdims=True)
+        left = jnp.sum(jnp.where(rank == lanes - 1, col, 0), axis=0, keepdims=True)
+        listed[1, 0:1, :] = jnp.sum(jnp.where(rank == lanes, subs, 0), axis=0, keepdims=True)
+        listed[1, 1:2, :] = ((here == left) & (lane > 0)).astype(jnp.int32)
+        copy = pltpu.make_async_copy(listed.at[1], order.at[1], order_sem.at[1])
+        copy.start()
+        running[slots] = jnp.zeros((tile, tile), jnp.float32)
+        copy.wait()
+
+    def col_pass(reduce, transform, first=False):
         def group(i, _):
+            if first:
+                tile_copy(i).wait()
             for u in range(unroll):
                 s = i * unroll + u
-                block = transform(tiles_ref[s] * rowmat[tr_ref[s]])
-                colpart[pl.ds(s, 1), :] = reduce(block, axis=0, keepdims=True)
+                block = tiles_ref[s] if first else tiles_ref[s] * rowmat[tr_ref[s]]
+                colpart[pl.ds(s, 1), :] = reduce(transform(block), axis=0, keepdims=True)
             return 0
 
         lax.fori_loop(0, slots // unroll, group, 0)
 
-    def row_pass(reduce, transform, combine):
-        lanes = lax.broadcasted_iota(jnp.int32, (tile, tile), 1)
-
+    def row_pass(reduce, transform, combine, first=False):
         def group(i, total):
             for u in range(unroll):
-                s = i * unroll + u
-                block = transform(tiles_ref[s] * colvec[pl.ds(tc_ref[s], 1), :])
-                total = jnp.where(lanes == s, reduce(block, axis=1, keepdims=True), total)
+                j = i * unroll + u
+                s = order[1, 0, j]
+                block = tiles_ref[s]
+                if not first:
+                    block = block * colvec[pl.ds(tc_ref[s], 1), :]
+                total = jnp.where(order[1, 1, j] == 1, total, 0.0)
+                total = combine(total, transform(block))
+                running[j] = total
             return total
 
-        total = lax.fori_loop(
-            0, slots // unroll, group, jnp.zeros((tile, tile), jnp.float32)
-        )
-        rowpart[...] = jnp.transpose(total)
-        ids = lax.broadcasted_iota(jnp.int32, (row_blocks, tile), 0)
-
-        def place(i, total):
-            for u in range(unroll):
-                s = i * unroll + u
-                at = jnp.where(s < count, tr_ref[s], -1)
-                part = rowpart[pl.ds(s, 1), :]
-                total = combine(total, jnp.where(ids == at, part, 0.0))
-            return total
-
-        return lax.fori_loop(
-            0, slots // unroll, place, jnp.zeros((row_blocks, tile), jnp.float32)
-        )
+        lax.fori_loop(0, slots // unroll, group, jnp.zeros((tile, tile), jnp.float32))
+        lanes = lax.broadcasted_iota(jnp.int32, (tile, tile), 1)
+        total = jnp.zeros((tile, tile), jnp.float32)
+        for r in range(row_blocks):
+            part = reduce(running[order[1, 2, r]], axis=1, keepdims=True)
+            total = jnp.where(lanes == r, part, total)
+        return jnp.transpose(total)[0:row_blocks]
 
     def plain(block):
         return block
@@ -243,17 +330,20 @@
 
     row_scale = jnp.ones((row_blocks, tile), jnp.float32)
     col_scale = jnp.ones((own, tile), jnp.float32)
-    colvec[...] = jnp.ones((col_blocks, tile), jnp.float32)
+    small[0].wait()
+    small[1].wait()
+    sort_slots()
     for sweep in range(RUIZ):
-        set_rows(row_scale)
-        col_pass(jnp.max, jnp.abs)
+        if sweep > 0:
+            set_rows(row_scale)
+        col_pass(jnp.max, jnp.abs, sweep == 0)
         scatter_cols(sweep, jnp.maximum, none)
         if sweep == 0:
             pl.semaphore_wait(barrier, n_row + n_col - 2)
         send_rs(sweep)
         if sweep > 0:
             take_ag(sweep - 1)
-        row_local = row_pass(jnp.max, jnp.abs, jnp.maximum)
+        row_local = row_pass(jnp.max, jnp.abs, jnp.maximum, sweep == 0)
         send_pair(sweep, row_local, none)
         col_peak = take_rs(sweep, jnp.maximum)[0] * col_scale
         col_scale = col_scale / jnp.sqrt(col_peak + EPS)
@@ -261,6 +351,8 @@
         row_peak = take_pair(sweep, jnp.maximum)[0] * row_scale
         row_scale = row_scale / jnp.sqrt(row_peak + EPS)
 
+    for copy in small[2:]:
+        copy.wait()
     rscale_out[...] = row_scale
     rhs_scaled = row_scale * rhs_ref[...]
     dual = dual_ref[...] / row_scale
@@ -370,6 +462,7 @@
     col_blocks = cost.shape[0] // tile
     own = col_blocks // n_row
     phases = RUIZ + ITERS
+    hbm = pl.BlockSpec(memory_space=pltpu.HBM)
     smem = pl.BlockSpec(memory_space=pltpu.SMEM)
     vmem = pl.BlockSpec(memory_space=pltpu.VMEM)
     f32 = jnp.float32
@@ -390,13 +483,28 @@
             jax.ShapeDtypeStruct((col_blocks, tile), f32),
             jax.ShapeDtypeStruct((1, 1), f32),
         ),
-        in_specs=[smem] * 4 + [vmem] * 7,
+        in_specs=[smem] * 2 + [hbm] * 9,
         out_specs=(vmem,) * 5,
         scratch_shapes=[
+            pltpu.SMEM((slots,), jnp.int32),
+            pltpu.SMEM((slots,), jnp.int32),
+            pltpu.VMEM((slots, tile, tile), f32),
+            pltpu.VMEM((col_blocks, tile), f32),
+            pltpu.VMEM((col_blocks, tile), f32),
+            pltpu.VMEM((col_blocks, tile), f32),
+            pltpu.VMEM((row_blocks, tile), f32),
+            pltpu.VMEM((col_blocks, tile), f32),
+            pltpu.VMEM((row_blocks, tile), f32),
+            dma((8,)),
+            dma((slots,)),
+            pltpu.VMEM((2, 8, tile), jnp.int32),
+            pltpu.SMEM((2, 8, tile), jnp.int32),
+            dma((2,)),
+            pltpu.VMEM((2, tile, tile), jnp.int32),
+            pltpu.VMEM((slots + 1, tile, tile), f32),
             pltpu.VMEM((row_blocks, tile, tile), f32),
             pltpu.VMEM((col_blocks, tile), f32),
             pltpu.VMEM((slots, tile), f32),
-            pltpu.VMEM((tile, tile), f32),
             pltpu.VMEM((phases, n_row, own + SIDE, tile), f32),
             pltpu.VMEM((phases, n_row, own + SIDE, tile), f32),
             pltpu.VMEM((phases, n_row, own + SIDE, tile), f32),
@@ -412,14 +520,14 @@
             dma((n_row,)),
         ],
         compiler_params=pltpu.CompilerParams(
-            collective_id=0, has_side_effects=True, vmem_limit_bytes=40 * 1024 * 1024
+            collective_id=0, has_side_effects=True, vmem_limit_bytes=63 * 1024 * 1024
         ),
         name="equilibrate_and_iterate",
     )(
+        counts,
+        step_start,
         tile_rows,
         tile_cols,
-        counts,
-        step_start,
         tiles,
         cols(cost),
         cols(lower),

time: 88.8 us -> 75.5 us (0.85)
  Pallas kernels: 73.3 us -> 66 us
  local copies, waits for them, and re-layouts: 11.3 us -> 5.54 us
    pallas_call x1, Pallas kernels: 73.3 us -> 66 us  [body(): pl.pallas_call(functools.partial(kernel, n_row, n_col), out_shape=(jax.Sh...]
    unnamed x22 -> x4, local copies, waits for them, and re-layouts: 11.3 us -> 5.54 us
where the time goes in v2:
time: 75.5 us; the launch traced here: 75.2 us
  Pallas kernels  66 us (87%)
  local copies, waits for them, and re-layouts  5.54 us (7%)
  between operations  3.7 us (5%)
    pallas_call x1, Pallas kernels, body(): pl.pallas_call(functools.partial(kernel, n_row, n_col), out_shape=(jax.Sh...  66 us
    unnamed x4, local copies, waits for them, and re-layouts  5.54 us

profile of v2, /device:TPU:0, one launch (start us, length us, event | category | flops | bytes accessed | tf_op | source)
XLA Modules:
  0.0 75.2 jit_solution(7814179880146363844)
XLA Ops:
  1.9 66.0 %equilibrate_and_iterate.1 = (f32[128,128]{1,0:T(8,128)}, f32[16,128]{1,0:T(8,128)}, f32[16,128]{1,0:T(8,128)}, f32[128,128]{1,0:T(8,128)}, f32[1,1]{1,0:T(1,128)}) custom-call(s32[1]{0:T(128)S(6)} %copy.21.count_ref, f32[1]{0:T(128)S(6)} %copy.22.step_ref, s32[96]{0:T(128)} %tr_hbm.1, s32[96]{0:T(128)} %tc_hbm.1, f32[96,128,128]{2,1,0:T(8,128)} %tiles_hbm.1, ...), custom_call_target="tpu_custom_call" | custom-call | tf_op jit(solution)/shard_map/equilibrate_and_iterate/pallas_call | solution.py:477
  67.9 1.5 %copy.23 = f32[16384]{0:T(1024)} copy(f32[16384]{0:T(1024)} %bitcast.16) | data formatting | bytes 131072
  69.4 1.3 %copy.24 = f32[2048]{0:T(1024)} copy(f32[2048]{0:T(1024)} %bitcast.20) | data formatting | bytes 16384
  70.7 1.3 %copy.25 = f32[2048]{0:T(1024)} copy(f32[2048]{0:T(1024)} %bitcast.19) | data formatting | bytes 16384
  72.0 1.5 %copy.26 = f32[16384]{0:T(1024)} copy(f32[16384]{0:T(1024)} %bitcast.15) | data formatting | bytes 131072

commit v3 on v2

--- a/solution.py
+++ b/solution.py
@@ -190,7 +190,10 @@
         owners = next(p for p in (4, 2, 1) if n_row % p == 0)
         ids = lax.broadcasted_iota(jnp.int32, (owners * own, tile), 0)
 
-        def some(p, _):
+        groups = n_row // owners
+
+        def some(i, _):
+            p = lax.rem(me // owners + 1 + i, groups)
             first = p * (owners * own)
 
             def group(i, total):
@@ -210,13 +213,17 @@
                     rs_send[k, p * owners + q, own : own + SIDE] = jnp.broadcast_to(
                         side, (SIDE, tile)
                     )
+            for q in range(owners):
+                owner = p * owners + q
+
+                @pl.when(owner != me)
+                def _():
+                    rs_copy(k, owner, me).start()
+
             return 0
 
-        lax.fori_loop(0, n_row // owners, some, 0)
+        lax.fori_loop(0, groups, some, 0)
         rs_recv[k, me, 0 : length(k)] = rs_send[k, me, 0 : length(k)]
-
-    def send_rs(k):
-        over_peers(lambda peer: rs_copy(k, peer, me).start())
 
     def take_rs(k, combine):
         over_peers(lambda peer: rs_copy(k, peer, peer).wait_recv())
@@ -332,16 +339,16 @@
     col_scale = jnp.ones((own, tile), jnp.float32)
     small[0].wait()
     small[1].wait()
-    sort_slots()
     for sweep in range(RUIZ):
         if sweep > 0:
             set_rows(row_scale)
         col_pass(jnp.max, jnp.abs, sweep == 0)
+        if sweep == 0:
+            pl.semaphore_wait(barrier, n_row + n_col - 2)
         scatter_cols(sweep, jnp.maximum, none)
         if sweep == 0:
-            pl.semaphore_wait(barrier, n_row + n_col - 2)
-        send_rs(sweep)
-        if sweep > 0:
+            sort_slots()
+        else:
             take_ag(sweep - 1)
         row_local = row_pass(jnp.max, jnp.abs, jnp.maximum, sweep == 0)
         send_pair(sweep, row_local, none)
@@ -359,7 +366,6 @@
     set_rows(row_scale * dual)
     col_pass(jnp.sum, plain)
     scatter_cols(RUIZ, add, total_of(rhs_scaled * rhs_scaled))
-    send_rs(RUIZ)
 
     take_ag(RUIZ - 1)
     whole_scale = colvec[...]
@@ -412,7 +418,6 @@
             set_rows(row_scale * dual)
             col_pass(jnp.sum, plain)
             scatter_cols(RUIZ + 1 + k, add, both)
-            send_rs(RUIZ + 1 + k)
         else:
             last_recv[me] = both
             over_peers(lambda peer: last_copy(peer, me).start())
@@ -432,6 +437,18 @@
         for step in range(1, n_col):
             pair_copy(k, lax.rem(core + step, n_col), core).wait_send()
     over_peers(lambda peer: last_copy(peer, me).wait_send())
+
+
+def deliver(*refs):
+    sources, targets, sem = refs[:4], refs[4:8], refs[8]
+    copies = [
+        pltpu.make_async_copy(source, target, sem.at[i])
+        for i, (source, target) in enumerate(zip(sources, targets))
+    ]
+    for copy in copies:
+        copy.start()
+    for copy in copies:
+        copy.wait()
 
 
 def next_step(k, eta, weight, primal_sq, side):
@@ -536,6 +553,16 @@
         cols(primal_start),
         rows(dual_start),
     )
+    results = (primal, dual, row_scale, col_scale)
+    primal, dual, row_scale, col_scale = pl.pallas_call(
+        deliver,
+        out_shape=tuple(jax.ShapeDtypeStruct(x.shape, f32) for x in results),
+        in_specs=[hbm] * 4,
+        out_specs=(hbm,) * 4,
+        scratch_shapes=[dma((4,))],
+        compiler_params=pltpu.CompilerParams(vmem_limit_bytes=63 * 1024 * 1024),
+        name="deliver",
+    )(*results)
     return (
         primal.reshape(-1),
         dual.reshape(-1),

time: 75.5 us -> 72.2 us (0.956)
  local copies, waits for them, and re-layouts: 5.54 us -> 0 us
  Pallas kernels: 66 us -> 68.3 us
    pallas_call x0 -> x1, Pallas kernels: none -> 5.61 us  [body(): pl.pallas_call(deliver, out_shape=tuple((jax.ShapeDtypeStruct(x.shape, f3...]
    unnamed x4 -> x0, local copies, waits for them, and re-layouts: 5.54 us -> none
    pallas_call x1, Pallas kernels: 66 us -> 62.7 us  [body(): pl.pallas_call(functools.partial(kernel, n_row, n_col), out_shape=(jax.Sh...]
where the time goes in v3:
time: 72.2 us; the launch traced here: 72 us
  Pallas kernels  68.3 us (95%)
  between operations  3.69 us (5%)
    pallas_call x1, Pallas kernels, body(): pl.pallas_call(functools.partial(kernel, n_row, n_col), out_shape=(jax.Sh...  62.7 us
    pallas_call x1, Pallas kernels, body(): pl.pallas_call(deliver, out_shape=tuple((jax.ShapeDtypeStruct(x.shape, f3...  5.61 us

profile of v3, /device:TPU:0, one launch (start us, length us, event | category | flops | bytes accessed | tf_op | source)
XLA Modules:
  0.0 72.0 jit_solution(3625773483798698400)
XLA Ops:
  1.9 62.7 %equilibrate_and_iterate.1 = (f32[128,128]{1,0:T(8,128)}, f32[16,128]{1,0:T(8,128)}, f32[16,128]{1,0:T(8,128)}, f32[128,128]{1,0:T(8,128)}, f32[1,1]{1,0:T(1,128)}) custom-call(s32[1]{0:T(128)S(6)} %copy.17.count_ref, f32[1]{0:T(128)S(6)} %copy.18.step_ref, s32[96]{0:T(128)} %tr_hbm.1, s32[96]{0:T(128)} %tc_hbm.1, f32[96,128,128]{2,1,0:T(8,128)} %tiles_hbm.1, ...), custom_call_target="tpu_custom_call" | custom-call | tf_op jit(solution)/shard_map/equilibrate_and_iterate/pallas_call | solution.py:494
  64.6 5.6 %deliver.1 = (f32[128,128]{1,0:T(8,128)}, f32[16,128]{1,0:T(8,128)}, f32[16,128]{1,0:T(8,128)}, f32[128,128]{1,0:T(8,128)}) custom-call(f32[128,128]{1,0:T(8,128)} %get-tuple-element.14.refs_0_, f32[16,128]{1,0:T(8,128)} %get-tuple-element.15.refs_1_, f32[16,128]{1,0:T(8,128)} %get-tuple-element.16.refs_2_, f32[128,128]{1,0:T(8,128)} %get-tuple-element.17.refs_3_), custom_call_target="tpu_custom_call" | custom-call | tf_op jit(solution)/shard_map/deliver/pallas_call | solution.py:557

commit v4 on v3

--- a/solution.py
+++ b/solution.py
@@ -28,10 +28,10 @@
     rhs_hbm,
     primal_hbm,
     dual_hbm,
-    primal_out,
-    dual_out,
-    rscale_out,
-    cscale_out,
+    primal_to,
+    dual_to,
+    rscale_to,
+    cscale_to,
     step_out,
     tr_ref,
     tc_ref,
@@ -65,6 +65,11 @@
     pair_rsem,
     last_ssem,
     last_rsem,
+    primal_out,
+    dual_out,
+    rscale_out,
+    cscale_out,
+    out_sem,
 ):
     slots, tile, _ = tiles_ref.shape
     row_blocks = rhs_ref.shape[0]
@@ -89,6 +94,18 @@
                 (rhs_hbm, rhs_ref),
                 (primal_hbm, primal_ref),
                 (dual_hbm, dual_ref),
+            ]
+        )
+    ]
+
+    outward = [
+        pltpu.make_async_copy(source, target, out_sem.at[i])
+        for i, (source, target) in enumerate(
+            [
+                (primal_out, primal_to),
+                (dual_out, dual_to),
+                (rscale_out, rscale_to),
+                (cscale_out, cscale_to),
             ]
         )
     ]
@@ -361,6 +378,7 @@
     for copy in small[2:]:
         copy.wait()
     rscale_out[...] = row_scale
+    outward[2].start()
     rhs_scaled = row_scale * rhs_ref[...]
     dual = dual_ref[...] / row_scale
     set_rows(row_scale * dual)
@@ -370,6 +388,7 @@
     take_ag(RUIZ - 1)
     whole_scale = colvec[...]
     cscale_out[...] = whole_scale
+    outward[3].start()
     whole_cost = whole_scale * cost_ref[...]
     colvec[...] = whole_scale * (primal_ref[...] / whole_scale)
     send_pair(RUIZ, row_pass(jnp.sum, plain, add), total_of(whole_cost * whole_cost))
@@ -422,7 +441,15 @@
             last_recv[me] = both
             over_peers(lambda peer: last_copy(peer, me).start())
             primal_out[...] = colvec[...]
+            outward[0].start()
             dual_out[...] = row_scale * dual
+            outward[1].start()
+            for m in range(RUIZ + ITERS):
+                over_peers(lambda peer: rs_copy(m, peer, me).wait_send())
+                over_peers(lambda peer: ag_copy(m, peer, me).wait_send())
+            for m in range(RUIZ + ITERS + 1):
+                for step in range(1, n_col):
+                    pair_copy(m, lax.rem(core + step, n_col), core).wait_send()
             over_peers(lambda peer: last_copy(peer, peer).wait_recv())
             side = last_recv[0]
             for p in range(1, n_row):
@@ -430,24 +457,22 @@
             eta = next_step(k, eta, weight, before, side)
     step_out[...] = eta[:, 0:1]
 
-    for k in range(RUIZ + ITERS):
-        over_peers(lambda peer: rs_copy(k, peer, me).wait_send())
-        over_peers(lambda peer: ag_copy(k, peer, me).wait_send())
-    for k in range(RUIZ + ITERS + 1):
-        for step in range(1, n_col):
-            pair_copy(k, lax.rem(core + step, n_col), core).wait_send()
     over_peers(lambda peer: last_copy(peer, me).wait_send())
+    for copy in outward:
+        copy.wait()
 
 
 def deliver(*refs):
-    sources, targets, sem = refs[:4], refs[4:8], refs[8]
-    copies = [
-        pltpu.make_async_copy(source, target, sem.at[i])
-        for i, (source, target) in enumerate(zip(sources, targets))
-    ]
-    for copy in copies:
+    sources, targets, stages = refs[:4], refs[4:8], refs[8:12]
+    in_sem, out_sem = refs[12:]
+    inward = [pltpu.make_async_copy(sources[i], stages[i], in_sem.at[i]) for i in range(4)]
+    outward = [pltpu.make_async_copy(stages[i], targets[i], out_sem.at[i]) for i in range(4)]
+    for copy in inward:
         copy.start()
-    for copy in copies:
+    for i in range(4):
+        inward[i].wait()
+        outward[i].start()
+    for copy in outward:
         copy.wait()
 
 
@@ -501,7 +526,7 @@
             jax.ShapeDtypeStruct((1, 1), f32),
         ),
         in_specs=[smem] * 2 + [hbm] * 9,
-        out_specs=(vmem,) * 5,
+        out_specs=(hbm,) * 4 + (vmem,),
         scratch_shapes=[
             pltpu.SMEM((slots,), jnp.int32),
             pltpu.SMEM((slots,), jnp.int32),
@@ -535,6 +560,11 @@
             dma((phases + 1, n_col)),
             dma((n_row,)),
             dma((n_row,)),
+            pltpu.VMEM((col_blocks, tile), f32),
+            pltpu.VMEM((row_blocks, tile), f32),
+            pltpu.VMEM((row_blocks, tile), f32),
+            pltpu.VMEM((col_blocks, tile), f32),
+            dma((4,)),
         ],
         compiler_params=pltpu.CompilerParams(
             collective_id=0, has_side_effects=True, vmem_limit_bytes=63 * 1024 * 1024
@@ -559,7 +589,7 @@
         out_shape=tuple(jax.ShapeDtypeStruct(x.shape, f32) for x in results),
         in_specs=[hbm] * 4,
         out_specs=(hbm,) * 4,
-        scratch_shapes=[dma((4,))],
+        scratch_shapes=[pltpu.VMEM(x.shape, f32) for x in results] + [dma((4,)), dma((4,))],
         compiler_params=pltpu.CompilerParams(vmem_limit_bytes=63 * 1024 * 1024),
         name="deliver",
     )(*results)

time: 72.2 us -> 67.3 us (0.932)
  Pallas kernels: 68.3 us -> 63.4 us
    pallas_call x1, Pallas kernels: 5.61 us -> 1.6 us  [body(): pl.pallas_call(deliver, out_shape=tuple((jax.ShapeDtypeStruct(x.shape, f3...]
    pallas_call x1, Pallas kernels: 62.7 us -> 61.8 us  [body(): pl.pallas_call(functools.partial(kernel, n_row, n_col), out_shape=(jax.Sh...]
where the time goes in v4:
time: 67.3 us; the launch traced here: 67.1 us
  Pallas kernels  63.4 us (94%)
  between operations  3.69 us (5%)
    pallas_call x1, Pallas kernels, body(): pl.pallas_call(functools.partial(kernel, n_row, n_col), out_shape=(jax.Sh...  61.8 us
    pallas_call x1, Pallas kernels, body(): pl.pallas_call(deliver, out_shape=tuple((jax.ShapeDtypeStruct(x.shape, f3...  1.6 us

profile of v4, /device:TPU:0, one launch (start us, length us, event | category | flops | bytes accessed | tf_op | source)
XLA Modules:
  0.0 67.1 jit_solution(3293742725319635611)
XLA Ops:
  1.9 61.8 %equilibrate_and_iterate.1 = (f32[128,128]{1,0:T(8,128)}, f32[16,128]{1,0:T(8,128)}, f32[16,128]{1,0:T(8,128)}, f32[128,128]{1,0:T(8,128)}, f32[1,1]{1,0:T(1,128)}) custom-call(s32[1]{0:T(128)S(6)} %copy.17.count_ref, f32[1]{0:T(128)S(6)} %copy.18.step_ref, s32[96]{0:T(128)} %tr_hbm.1, s32[96]{0:T(128)} %tc_hbm.1, f32[96,128,128]{2,1,0:T(8,128)} %tiles_hbm.1, ...), custom_call_target="tpu_custom_call" | custom-call | tf_op jit(solution)/shard_map/equilibrate_and_iterate/pallas_call | solution.py:519
  63.7 1.6 %deliver.1 = (f32[128,128]{1,0:T(8,128)}, f32[16,128]{1,0:T(8,128)}, f32[16,128]{1,0:T(8,128)}, f32[128,128]{1,0:T(8,128)}) custom-call(f32[128,128]{1,0:T(8,128)} %get-tuple-element.14.refs_0_, f32[16,128]{1,0:T(8,128)} %get-tuple-element.15.refs_1_, f32[16,128]{1,0:T(8,128)} %get-tuple-element.16.refs_2_, f32[128,128]{1,0:T(8,128)} %get-tuple-element.17.refs_3_), custom_call_target="tpu_custom_call" | custom-call | tf_op jit(solution)/shard_map/deliver/pallas_call | solution.py:587
